TPU v7x, 512 devices: a whole 4x8x8 slice. The times are simulated.
512 devices in a mesh: seq: 64 (over z_lo, x, y), kv: 8 (over z_hi, core).
Axes of the slice: x: 4, y: 8, z: 8 (z_hi: 4, z_lo: 2; z = z_hi * 2 + z_lo), core: 2. Of those that a mesh axis runs over, the one named last changes fastest.
Arguments:
- text_query: bfloat16 [8192, 8192], P('seq', 'kv'), may hold values from -20 to 20, as said below
- vision_key: bfloat16 [2048, 1024], P('seq', 'kv'), may hold values from -4 to 4, as said below
- vision_value: bfloat16 [2048, 1024], P('seq', 'kv'), may hold values from -6 to 6
- grad_output: bfloat16 [8192, 8192], P('seq', 'kv'), may hold values from -192 to 192
- key_weight: bfloat16 [8192, 1024], P('seq', 'kv'), may hold values from -0.1875 to 0.1875
- value_weight: bfloat16 [8192, 1024], P('seq', 'kv'), may hold values from -0.1875 to 0.1875
Outputs:
- grad_query: bfloat16 [8192, 8192], P('seq', 'kv')
- grad_vision: bfloat16 [2048, 8192], P('seq', 'kv')
Inputs may be any that keep to these rules, and one draw needn't show every extreme that they name: `text_query`: entries of order one; some rows of single heads may be large multiples of a key row. `vision_key`: entries of order one.
All inputs are finite; a program needn't handle non-finite values.
Results may differ from a plain program's by a relative error of at most 0.02.
Values may be sent and summed in bfloat16 or wider, within the bound.
A program may use at most 64 MiB of HBM per device.

v0:
```python
import math

import jax
import jax.numpy as jnp
from jax import lax
from jax.sharding import PartitionSpec as P

HEAD = 128


def sweep(block_step, running, shard_piece):
    key_part, value_part = shard_piece
    key_count = key_part.shape[0]
    block_rows = 512
    num_blocks = key_count // block_rows
    key_blocks = key_part.reshape(num_blocks, block_rows, key_part.shape[1])
    value_blocks = value_part.reshape(num_blocks, block_rows, value_part.shape[1])

    def inner(inner_state, inputs):
        key_block, value_block, block_index = inputs
        return (block_step(inner_state, key_block, value_block, block_index * block_rows), None)

    result, unused = lax.scan(
        inner, running, (key_blocks, value_blocks, jnp.arange(num_blocks, dtype=jnp.int32))
    )
    return result


def shards(text_query, vision_key, vision_value, grad_output, key_weight, value_weight):
    scaling = 1.0 / math.sqrt(HEAD)
    row_count = text_query.shape[0]
    head_count = text_query.shape[1] // HEAD
    queries = text_query.reshape(row_count, head_count, HEAD)
    upstream = grad_output.reshape(row_count, head_count, HEAD)
    shard_keys = vision_key.shape[0]
    total_keys = shard_keys * lax.axis_size("seq")

    def logit_pair(key_block, value_block):
        logits = (
            jnp.einsum("thd,kd->htk", queries, key_block, preferred_element_type=jnp.float32)
            * scaling
        )
        grad_probs = jnp.einsum(
            "thd,kd->htk", upstream, value_block, preferred_element_type=jnp.float32
        )
        return (logits, grad_probs)

    def stats_block(running, key_block, value_block, offset):
        row_max, row_sums, weighted = running
        logits, grad_probs = logit_pair(key_block, value_block)
        new_max = jnp.maximum(row_max, jnp.max(logits, axis=2))
        exponent = jnp.exp(logits - new_max[:, :, None])
        factor = jnp.exp(row_max - new_max)
        return (
            new_max,
            row_sums * factor + jnp.sum(exponent, axis=2),
            weighted * factor + jnp.sum(exponent * grad_probs, axis=2),
        )

    init_stats = (
        jnp.full((head_count, row_count), -jnp.inf, jnp.float32),
        jnp.zeros((head_count, row_count), jnp.float32),
        jnp.zeros((head_count, row_count), jnp.float32),
    )

    def make_grads(stats):
        row_max, row_sums, weighted = stats
        row_dots = weighted / row_sums

        def attend(key_block, value_block):
            logits, grad_probs = logit_pair(key_block, value_block)
            attention = jnp.exp(logits - row_max[:, :, None]) / row_sums[:, :, None]
            grad_logits = (attention * (grad_probs - row_dots[:, :, None]) * scaling).astype(
                jnp.bfloat16
            )
            return (attention, grad_logits)

        def block_terms(attention, grad_logits):
            value_term = jnp.einsum(
                "htk,thd->kd",
                attention.astype(jnp.bfloat16),
                upstream,
                preferred_element_type=jnp.float32,
            )
            key_term = jnp.einsum(
                "htk,thd->kd", grad_logits, queries, preferred_element_type=jnp.float32
            )
            return jnp.concatenate([key_term, value_term], axis=1)

        def grad_block(running, key_block, value_block, offset):
            query_grad, key_grads = running
            attention, grad_logits = attend(key_block, value_block)
            query_grad = query_grad + jnp.einsum(
                "htk,kd->thd", grad_logits, key_block, preferred_element_type=jnp.float32
            )
            key_grads = lax.dynamic_update_slice(
                key_grads, block_terms(attention, grad_logits), (offset, jnp.int32(0))
            )
            return (query_grad, key_grads)

        def query_block(query_grad, key_block, value_block, offset):
            attention, grad_logits = attend(key_block, value_block)
            return query_grad + jnp.einsum(
                "htk,kd->thd", grad_logits, key_block, preferred_element_type=jnp.float32
            )

        return (attend, block_terms, grad_block, query_block)

    init_query = jnp.zeros((row_count, head_count, HEAD), jnp.float32)
    init_grads = (init_query, jnp.zeros((total_keys, 2 * HEAD), jnp.float32))
    keys_all, values_all = (
        lax.all_gather(vision_key, "seq", axis=0, tiled=True),
        lax.all_gather(vision_value, "seq", axis=0, tiled=True),
    )
    stats = sweep(stats_block, init_stats, (keys_all, values_all))
    attend, block_terms, grad_block, query_block = make_grads(stats)
    query_grad, key_grads = sweep(grad_block, init_grads, (keys_all, values_all))
    owned_sums = lax.psum_scatter(key_grads, "seq", scatter_dimension=0, tiled=True)
    owned_grads = owned_sums.astype(jnp.bfloat16)
    merged_weights = jnp.concatenate([key_weight, value_weight], axis=1)
    vision_terms = jnp.einsum(
        "kc,rc->kr",
        owned_grads,
        lax.all_gather(merged_weights, "seq", axis=0, tiled=True),
        preferred_element_type=jnp.float32,
    )
    grad_vision = lax.psum_scatter(
        vision_terms.astype(jnp.bfloat16), "kv", scatter_dimension=1, tiled=True
    )
    grad_query = query_grad.reshape(row_count, head_count * HEAD).astype(jnp.bfloat16)
    return (grad_query, grad_vision)


def solution(mesh):
    return jax.shard_map(
        shards,
        mesh=mesh,
        in_specs=(
            P("seq", "kv"),
            P("seq", "kv"),
            P("seq", "kv"),
            P("seq", "kv"),
            P("seq", "kv"),
            P("seq", "kv"),
        ),
        out_specs=(P("seq", "kv"), P("seq", "kv")),
        check_vma=False,
    )
```

profile of v0, /device:TPU:6, one launch (start us, length us, event | category | flops | bytes accessed | tf_op | source)
XLA Modules:
  0.0 1057.5 jit_solution(18121476715610056676)
XLA Ops:
  7.2 0.0 reduce-scatter.7.cloned.1.call-start
  7.3 151.4 %all_gather.9 = bf16[2048,128]{1,0:T(8,128)(2,1)} all-gather(bf16[32,128]{1,0:T(8,128)(2,1)} %param.11), channel_id=1, replica_groups=mesh['seq'=64,'kv'=8] {'seq'}, dimensions={0}, use_global_device_ids=true | all-gather | bytes 532480 | tf_op jit(solution)/shard_map/all_gather | solution.py:112
  158.7 164.4 %all_gather.10 = bf16[2048,128]{1,0:T(8,128)(2,1)} all-gather(bf16[32,128]{1,0:T(8,128)(2,1)} %param.12), channel_id=1, replica_groups=mesh['seq'=64,'kv'=8] {'seq'}, dimensions={0}, use_global_device_ids=true | all-gather | bytes 532480 | tf_op jit(solution)/shard_map/all_gather | solution.py:113
  323.1 1.1 copy.25
  324.2 0.2 copy.27
  324.4 0.2 copy.26
  324.6 0.9 copy.28
  325.5 13.4 %while.28 = (s32[]{:T(128)}, f32[8,128]{1,0:T(8,128)S(1)}, f32[8,128]{1,0:T(8,128)S(1)}, f32[8,128]{1,0:T(8,128)S(1)}, bf16[4,512,128]{2,1,0:T(8,128)(2,1)}, /*i...) while((s32[]{:T(128)}, f32[8,128]{1,0:T(8,128)S(1)}, ...), condition=%wide.region_4.5_spmd.clone, body=%wide.region_0.4_spmd.clone.sunk | while | flops 273161216 | bytes 7152752 | solution.py:23
  325.5 1.3 bitcast_reduce_fusion.2
  326.8 1.6 fusion.61
  328.4 0.4 fusion.62
  328.8 1.3 bitcast_reduce_fusion.2
  330.2 1.6 fusion.61
  331.8 0.4 fusion.62
  332.2 1.3 bitcast_reduce_fusion.2
  333.5 1.6 fusion.61
  335.1 0.4 fusion.62
  335.5 1.3 bitcast_reduce_fusion.2
  336.9 1.6 fusion.61
  338.5 0.4 fusion.62
  338.9 1.5 broadcast_in_dim.14.clone
  340.4 29.6 %while.29 = (s32[]{:T(128)}, f32[128,8,128]{0,2,1:T(8,128)S(1)}, f32[2048,256]{1,0:T(8,128)}, bf16[4,512,128]{2,1,0:T(8,128)(2,1)}, bf16[128,8,128]{0,2,1:T(8,12...) while((s32[]{:T(128)}, f32[128,8,128]{0,2,1:T(8,128)S(1)}, ...), condition=%wide.region_6.7_spmd.clone, body=%wide.region_5.6_spmd.clone.sunk | while | flops 675676160 | bytes 15611605 | solution.py:23
  340.4 1.4 fusion.74
  341.8 1.3 fusion.75
  343.1 0.5 convolution_bitcast_fusion.6
  343.6 0.5 convolution_bitcast_fusion.5
  344.2 0.2 copy.43
  344.4 0.6 dynamic_slice.55
  345.6 0.8 constant_dynamic-update-slice_fusion.2
  346.4 1.3 fusion.76
  347.8 1.4 fusion.74
  349.2 1.3 fusion.75
  350.5 0.5 convolution_bitcast_fusion.6
  351.0 0.5 convolution_bitcast_fusion.5
  351.6 0.2 copy.43
  351.8 0.6 dynamic_slice.55
  353.0 0.8 constant_dynamic-update-slice_fusion.2
  353.9 1.3 fusion.76
  355.2 1.4 fusion.74
  356.6 1.3 fusion.75
  358.0 0.5 convolution_bitcast_fusion.6
  358.4 0.5 convolution_bitcast_fusion.5
  359.0 0.2 copy.43
  359.2 0.6 dynamic_slice.55
  360.4 0.8 constant_dynamic-update-slice_fusion.2
  361.3 1.3 fusion.76
  362.6 1.4 fusion.74
  364.0 1.3 fusion.75
  365.4 0.5 convolution_bitcast_fusion.6
  365.9 0.5 convolution_bitcast_fusion.5
  366.4 0.2 copy.43
  366.6 0.6 dynamic_slice.55
  367.8 0.8 constant_dynamic-update-slice_fusion.2
  368.7 1.3 fusion.76
  370.0 0.0 all-gather.2.cloned.1.call-start
  370.1 0.7 copy-done.1
  370.8 0.6 pad_maximum_fusion.1
  371.4 0.0 reduce-scatter.5.cloned.1.call-start
  371.5 318.2 %reduce-scatter.7.cloned.1.call-done = f32[32,256]{1,0:T(8,128)} async-done(((f32[2048,256]{1,0:T(8,128)}), f32[32,256]{1,0:T(8,128)}) %reduce-scatter.7.cloned.1.call-update) | async-done | bytes 32784
  689.7 0.9 copy.39
  690.6 305.7 %all-gather.2.cloned.1.call-done = bf16[8192,256]{1,0:T(8,128)(2,1)} async-done(((bf16[128,256]{1,0:T(8,128)(2,1)}), bf16[8192,256]{1,0:T(8,128)(2,1)}) %all-gather.2.cloned.1.call-update) | async-done | bytes 4194320 | tf_op jit(solution)/shard_map/all_gather | solution.py:124
  996.3 4.3 convolution_convert_fusion
  1000.7 0.9 copy.36
  1001.5 49.4 %reduce-scatter.5.cloned.1.call-done = bf16[32,1024]{1,0:T(8,128)(2,1)} async-done(((bf16[32,8192]{1,0:T(8,128)(2,1)}), bf16[32,1024]{1,0:T(8,128)(2,1)}) %reduce-scatter.5.cloned.1.call-update) | async-done | bytes 65552 | tf_op jit(solution)/shard_map/reduce_scatter | solution.py:127
  (31 shorter events, 0.4 us)
Async XLA Ops:
  7.2 317.2 %copy-start = (bf16[128,1024]{1,0:T(8,128)(2,1)S(1)}, bf16[128,1024]{1,0:T(8,128)(2,1)}, u32[]{:S(2)}) copy-start(bf16[128,1024]{1,0:T(8,128)(2,1)} %param.13) | copy-start | bytes 786436
  7.2 682.5 %reduce-scatter.7.cloned.1.call-start = ((), (), s32[]{:S(2)}) async-start(), calls=%async_computation.4 | async-start | bytes 2129920
  370.0 0.8 copy-start.1
  370.0 0.8 copy-start.2
  370.0 626.3 %all-gather.2.cloned.1.call-start = ((), (), s32[]{:S(2)}) async-start(), calls=%async_computation.2 | async-start | bytes 4259840 | tf_op jit(solution)/shard_map/all_gather | solution.py:124
  371.4 679.5 %reduce-scatter.5.cloned.1.call-start = ((), (), s32[]{:S(2)}) async-start(), calls=%async_computation.3 | async-start | bytes 589824 | tf_op jit(solution)/shard_map/reduce_scatter | solution.py:127
Sparse Core Ops, SparseCore 0:
  370.2 319.4 reduce-scatter.6
  692.6 303.6 all-gather.1
  1000.8 50.1 reduce-scatter.4
where the time goes:
time: 1060 us
  waiting for transfers between devices  673 us (63%)
  blocking collectives  316 us (30%)
  matrix products  36.1 us (3%)
  between operations  13.9 us (1%)
  local copies, waits for them, and re-layouts  12.7 us (1%)
    unnamed x4, waiting for transfers between devices  318 us
    all_gather x1, waiting for transfers between devices, shards(): lax.all_gather(merged_weights, 'seq', axis=0, tiled=True)  306 us
    all_gather x1, blocking collectives, shards(): lax.all_gather(vision_value, 'seq', axis=0, tiled=True)  164 us
    all_gather x1, blocking collectives, shards(): lax.all_gather(vision_key, 'seq', axis=0, tiled=True)  151 us
    reduce_scatter x1, waiting for transfers between devices, shards(): lax.psum_scatter(vision_terms.astype(jnp.bfloat16), 'kv', scatter_dimensi...  49.4 us
  transfers between devices with their start and end apart: 3, of which 3 were waited for; matrix products, arithmetic and copies ran while one was open for 0% of the time, Pallas kernels for 0%

commit v1 on v0

v1 whole, which is shorter than its diff:
```python
import math

import jax
import jax.numpy as jnp
from jax import lax
from jax.experimental import pallas as pl
from jax.experimental.pallas import tpu as pltpu
from jax.sharding import PartitionSpec as P

HEAD = 128
SCALING = 1.0 / math.sqrt(HEAD)
EXP2_SCALE = SCALING * math.log2(math.e)
LANES = 256
MESH = pl.DeviceIdType.MESH
F32 = jnp.float32
BF16 = jnp.bfloat16


def contract_last(a, b):
    return lax.dot_general(a, b, (((1,), (1,)), ((), ())), preferred_element_type=F32)


def kernel(
    sizes,
    query_ref, key_ref, value_ref, upstream_ref, key_weight_ref, value_weight_ref,
    grad_query_ref, grad_vision_ref,
    pairs, weights, query_rows, upstream_rows, query_t, upstream_t,
    exps, probs_grad, chunk_max, run_max, run_sum, run_dot,
    attn_low, logit_low, query_grad_t,
    term_send, term_recv, own_sum, row_send, row_recv, gathered,
    projected, sib_send, sib_recv, fin_send, fin_recv,
    gy_send, gy_recv, gu_send, gu_recv, wy_send, wy_recv,
    ru_send, ru_recv, ry_send, ry_recv, au_send, au_recv,
    sb_send, sb_recv, fn_send, fn_recv,
):
    nu, ny, nk = sizes
    block = key_ref.shape[0]
    chunk = block * ny
    tokens = query_ref.shape[0]
    heads = query_ref.shape[1] // HEAD
    rows = tokens * heads
    wblock = key_weight_ref.shape[0]
    half = nu // 2
    s = lax.axis_index("seq")
    g = lax.axis_index("kv")
    u, y = s // ny, s % ny
    core, pair = g % 2, g // 2
    diag = jnp.where(u == g, 1, 0)

    def at(u_, y_, g_):
        return {"seq": u_ * ny + y_, "kv": g_}

    def u_peer(d):
        return at((u + d) % nu, y, g)

    def y_peer(d):
        return at(u, (y + d) % ny, g)

    sibling = at(u, y, g + 1 - 2 * core)

    def remote(src, dst, send, recv, device):
        return pltpu.make_async_remote_copy(
            src_ref=src, dst_ref=dst, send_sem=send, recv_sem=recv,
            device_id=device, device_id_type=MESH,
        )

    barrier = pltpu.get_barrier_semaphore()

    def greet(device):
        pl.semaphore_signal(barrier, inc=1, device_id=device, device_id_type=MESH)

    @pl.loop(1, ny)
    def _(d):
        greet(y_peer(d))

    @pl.loop(1, nu)
    def _(d):
        greet(u_peer(d))

    greet(sibling)

    @pl.loop(0, nk // 2)
    def _(j):
        source = 2 * j + u % 2

        @pl.when(jnp.logical_not((u == g) & (source == g)))
        def _():
            greet(at(g, y, source))

    own_rows = pl.ds(pl.multiple_of(s * block, block), block)
    pairs[own_rows, :HEAD] = key_ref[...]
    pairs[own_rows, HEAD:] = value_ref[...]
    own_w = pl.ds(pl.multiple_of(y * wblock, wblock), wblock)
    weights[own_w, :HEAD] = key_weight_ref[...]
    weights[own_w, HEAD:] = value_weight_ref[...]
    for h in range(heads):
        at_cols = pl.ds(h * HEAD, HEAD)
        at_rows = pl.ds(h * tokens, tokens)
        q = query_ref[:, at_cols]
        o = upstream_ref[:, at_cols]
        query_rows[at_rows, :] = q
        upstream_rows[at_rows, :] = o
        query_t[:, at_rows] = q.T
        upstream_t[:, at_rows] = o.T
    run_max[...] = jnp.full_like(run_max, -1e30)
    run_sum[...] = jnp.zeros_like(run_sum)
    run_dot[...] = jnp.zeros_like(run_dot)
    query_grad_t[...] = jnp.zeros_like(query_grad_t)

    pl.semaphore_wait(barrier, (ny - 1) + (nu - 1) + 1 + half - diag)

    def gather_y(d):
        return remote(pairs.at[own_rows], pairs.at[own_rows], gy_send.at[d], gy_recv.at[d], y_peer(d))

    @pl.loop(1, ny)
    def _(d):
        gather_y(d).start()

    @pl.loop(1, ny)
    def _(d):
        gather_y(d).wait_recv()

    u_rows = pl.ds(pl.multiple_of(u * chunk, chunk), chunk)

    def gather_u(d):
        return remote(pairs.at[u_rows], pairs.at[u_rows], gu_send.at[d], gu_recv.at[d], u_peer(d))

    @pl.loop(1, nu)
    def _(d):
        gather_u(d).start()

    def gather_w(d):
        return remote(weights.at[own_w], weights.at[own_w], wy_send.at[d], wy_recv.at[d], y_peer(d))

    @pl.loop(1, ny)
    def _(d):
        gather_w(d).start()

    @pl.loop(0, nu)
    def _(d):
        @pl.when(d > 0)
        def _():
            gather_u(d).wait_recv()

        c = (u - d + nu) % nu
        at_c = pl.ds(pl.multiple_of(c * chunk, chunk), chunk)
        keys = pairs[at_c, :HEAD]
        values = pairs[at_c, HEAD:]
        for n in range(rows // LANES):
            cols = pl.ds(n * LANES, LANES)
            logits = jnp.dot(keys, query_t[:, cols], preferred_element_type=F32)
            gp = jnp.dot(values, upstream_t[:, cols], preferred_element_type=F32)
            old = run_max[:, cols]
            new = jnp.maximum(old, jnp.max(logits, axis=0, keepdims=True))
            factor = jnp.exp2((old - new) * EXP2_SCALE)
            e = jnp.exp2((logits - new) * EXP2_SCALE)
            run_max[:, cols] = new
            run_sum[:, cols] = run_sum[:, cols] * factor + jnp.sum(e, axis=0, keepdims=True)
            run_dot[:, cols] = run_dot[:, cols] * factor + jnp.sum(e * gp, axis=0, keepdims=True)
            exps[at_c, cols] = e
            probs_grad[at_c, cols] = gp
            chunk_max[c, :, cols] = new

    run_sum[...] = 1.0 / run_sum[...]
    run_dot[...] = run_dot[...] * run_sum[...]

    def reduce_u(d):
        return remote(term_send.at[d], term_recv.at[d], ru_send.at[d], ru_recv.at[d], u_peer(d))

    @pl.loop(1, nu + 1)
    def _(d):
        c = (u + d) % nu
        at_c = pl.ds(pl.multiple_of(c * chunk, chunk), chunk)
        for n in range(rows // LANES):
            cols = pl.ds(n * LANES, LANES)
            share = (
                jnp.exp2((chunk_max[c, :, cols] - run_max[:, cols]) * EXP2_SCALE)
                * run_sum[:, cols]
            )
            a = exps[at_c, cols] * share
            attn_low[:, cols] = a.astype(BF16)
            logit_low[:, cols] = (
                a * (probs_grad[at_c, cols] - run_dot[:, cols]) * SCALING
            ).astype(BF16)
        key_term = jnp.dot(logit_low[...], query_rows[...], preferred_element_type=F32)
        value_term = jnp.dot(attn_low[...], upstream_rows[...], preferred_element_type=F32)

        @pl.when(d < nu)
        def _():
            term_send[d, :, :HEAD] = key_term.astype(BF16)
            term_send[d, :, HEAD:] = value_term.astype(BF16)
            reduce_u(d).start()

        @pl.when(d == nu)
        def _():
            own_sum[:, :HEAD] = key_term
            own_sum[:, HEAD:] = value_term

        keys_t = pairs[at_c, :HEAD].T
        query_grad_t[...] += jnp.dot(keys_t, logit_low[...], preferred_element_type=F32)

    for h in range(heads):
        grad_query_ref[:, pl.ds(h * HEAD, HEAD)] = (
            query_grad_t[:, pl.ds(h * tokens, tokens)].T.astype(BF16)
        )

    @pl.loop(1, nu)
    def _(d):
        reduce_u(d).wait_recv()
        own_sum[...] += term_recv[d].astype(F32)

    def reduce_y(d):
        return remote(row_send.at[d], row_recv.at[d], ry_send.at[d], ry_recv.at[d], y_peer(d))

    def y_rows(d):
        return pl.ds(pl.multiple_of(((y + d) % ny) * block, block), block)

    @pl.loop(1, ny)
    def _(d):
        row_send[d] = own_sum[y_rows(d), :].astype(BF16)
        reduce_y(d).start()

    owned = own_sum[y_rows(0), :]
    for d in range(1, ny):
        reduce_y(d).wait_recv()
        owned += row_recv[d].astype(F32)
    gathered[u] = owned.astype(BF16)

    def spread_u(d):
        return remote(gathered.at[u], gathered.at[u], au_send.at[d], au_recv.at[d], u_peer(d))

    @pl.loop(1, nu)
    def _(d):
        spread_u(d).start()

    @pl.loop(1, ny)
    def _(d):
        gather_w(d).wait_recv()

    @pl.loop(1, nu)
    def _(d):
        spread_u(d).wait_recv()

    grads = gathered[...].reshape(nu * block, 2 * HEAD)
    for n in range(ny * wblock // LANES):
        cols = pl.ds(n * LANES, LANES)
        projected[:, cols] = contract_last(grads, weights[cols, :])

    def part(j, parity):
        return pl.ds(pl.multiple_of((2 * j + parity) * block, block), block)

    def swap(j):
        return remote(sib_send.at[j], sib_recv.at[j], sb_send.at[j], sb_recv.at[j], sibling)

    @pl.loop(0, half)
    def _(j):
        sib_send[j] = projected[part(j, 1 - core), :].astype(BF16)
        swap(j).start()

    def finish(j):
        return remote(
            fin_send.at[j], fin_recv.at[pair], fn_send.at[j], fn_recv.at[pair],
            at(2 * j + core, y, u),
        )

    def to_self(j):
        return (u == g) & (2 * j + core == u)

    @pl.loop(0, half)
    def _(j):
        swap(j).wait_recv()
        total = projected[part(j, core), :] + sib_recv[j].astype(F32)
        fin_send[j] = total.astype(BF16)

        @pl.when(jnp.logical_not(to_self(j)))
        def _():
            finish(j).start()

        @pl.when(to_self(j))
        def _():
            fin_recv[pair] = total.astype(BF16)

    @pl.loop(0, nk // 2)
    def _(j):
        @pl.when(jnp.logical_not((u == g) & (j == pair)))
        def _():
            remote(
                fin_send.at[0], fin_recv.at[j], fn_send.at[0], fn_recv.at[j], sibling
            ).wait_recv()

    result = fin_recv[0].astype(F32)
    for j in range(1, nk // 2):
        result += fin_recv[j].astype(F32)
    grad_vision_ref[...] = result.astype(BF16)

    @pl.loop(1, ny)
    def _(d):
        gather_y(d).wait_send()
        gather_w(d).wait_send()
        reduce_y(d).wait_send()

    @pl.loop(1, nu)
    def _(d):
        gather_u(d).wait_send()
        reduce_u(d).wait_send()
        spread_u(d).wait_send()

    @pl.loop(0, half)
    def _(j):
        swap(j).wait_send()

        @pl.when(jnp.logical_not(to_self(j)))
        def _():
            finish(j).wait_send()


def shards(sizes, text_query, vision_key, vision_value, grad_output, key_weight, value_weight):
    nu, ny, nk = sizes
    block = vision_key.shape[0]
    chunk = block * ny
    keys = chunk * nu
    tokens = text_query.shape[0]
    heads = text_query.shape[1] // HEAD
    rows = tokens * heads
    wide = key_weight.shape[0] * ny
    half = nu // 2
    vmem = pltpu.VMEM
    dma = pltpu.SemaphoreType.DMA
    return pl.pallas_call(
        lambda *refs: kernel(sizes, *refs),
        out_shape=(
            jax.ShapeDtypeStruct(text_query.shape, BF16),
            jax.ShapeDtypeStruct((block, wide), BF16),
        ),
        in_specs=[pl.BlockSpec(memory_space=pltpu.VMEM)] * 6,
        out_specs=(pl.BlockSpec(memory_space=pltpu.VMEM),) * 2,
        scratch_shapes=[
            vmem((keys, 2 * HEAD), BF16),
            vmem((wide, 2 * HEAD), BF16),
            vmem((rows, HEAD), BF16),
            vmem((rows, HEAD), BF16),
            vmem((HEAD, rows), BF16),
            vmem((HEAD, rows), BF16),
            vmem((keys, rows), F32),
            vmem((keys, rows), F32),
            vmem((nu, 1, rows), F32),
            vmem((1, rows), F32),
            vmem((1, rows), F32),
            vmem((1, rows), F32),
            vmem((chunk, rows), BF16),
            vmem((chunk, rows), BF16),
            vmem((HEAD, rows), F32),
            vmem((nu, chunk, 2 * HEAD), BF16),
            vmem((nu, chunk, 2 * HEAD), BF16),
            vmem((chunk, 2 * HEAD), F32),
            vmem((ny, block, 2 * HEAD), BF16),
            vmem((ny, block, 2 * HEAD), BF16),
            vmem((nu, block, 2 * HEAD), BF16),
            vmem((nu * block, wide), F32),
            vmem((half, block, wide), BF16),
            vmem((half, block, wide), BF16),
            vmem((half, block, wide), BF16),
            vmem((nk // 2, block, wide), BF16),
            dma((ny,)), dma((ny,)), dma((nu,)), dma((nu,)), dma((ny,)), dma((ny,)),
            dma((nu,)), dma((nu,)), dma((ny,)), dma((ny,)), dma((nu,)), dma((nu,)),
            dma((half,)), dma((half,)), dma((half,)), dma((nk // 2,)),
        ],
        compiler_params=pltpu.CompilerParams(
            collective_id=0, has_side_effects=True, vmem_limit_bytes=48 * 1024 * 1024
        ),
    )(text_query, vision_key, vision_value, grad_output, key_weight, value_weight)


def solution(mesh):
    nk = mesh.shape["kv"]
    sizes = (nk, mesh.shape["seq"] // nk, nk)
    spec = P("seq", "kv")
    return jax.shard_map(
        lambda *arrays: shards(sizes, *arrays),
        mesh=mesh,
        in_specs=(spec,) * 6,
        out_specs=(spec, spec),
        check_vma=False,
    )
```

time: 1060 us -> 82.9 us (0.08)
  the two profiles are of different devices: /device:TPU:6 before, /device:TPU:71 now
where the time goes in v1:
time: 82.9 us; the launch traced here: 82.5 us
  Pallas kernels  75.7 us (91%)
  local copies, waits for them, and re-layouts  6.13 us (7%)
    pallas_call x1, Pallas kernels, shards(): pl.pallas_call(lambda *refs: kernel(sizes, *refs), out_shape=(jax.ShapeDt...  75.7 us
    unnamed x14, local copies, waits for them, and re-layouts  6.13 us

profile of v1, /device:TPU:71, one launch (start us, length us, event | category | flops | bytes accessed | tf_op | source)
XLA Modules:
  0.0 82.5 jit_solution(1890985585674960687)
XLA Ops:
  0.6 0.0 copy-start
  0.6 0.9 %copy-done = bf16[128,1024]{1,0:T(8,128)(2,1)S(1)} copy-done((bf16[128,1024]{1,0:T(8,128)(2,1)S(1)}, bf16[128,1024]{1,0:T(8,128)(2,1)}, u32[]{:S(2)}) %copy-start) | copy-done | bytes 262168
  1.6 0.0 copy-start.1
  1.6 0.9 %copy-done.1 = bf16[128,1024]{1,0:T(8,128)(2,1)S(1)} copy-done((bf16[128,1024]{1,0:T(8,128)(2,1)S(1)}, bf16[128,1024]{1,0:T(8,128)(2,1)}, u32[]{:S(2)}) %copy-start.1) | copy-done | bytes 262168
  2.5 0.0 copy-start.2
  2.5 0.8 copy-done.2
  3.3 0.0 copy-start.3
  3.3 0.8 copy-done.3
  4.0 0.0 copy-start.4
  4.1 0.7 copy-done.4
  4.7 0.0 copy-start.5
  4.7 0.7 copy-done.5
  5.4 75.7 %shard_map.77 = (bf16[128,1024]{1,0:T(8,128)(2,1)S(1)}, bf16[32,1024]{1,0:T(8,128)(2,1)S(1)}) custom-call(bf16[128,1024]{1,0:T(8,128)(2,1)S(1)} %copy-done, bf16[32,128]{1,0:T(8,128)(2,1)S(1)} %copy-done.4, bf16[32,128]{1,0:T(8,128)(2,1)S(1)} %copy-done.5, bf16[128,1024]{1,0:T(8,128)(2,1)S(1)} %copy-done.1, bf16[128,128]{1,0:T(8,128)(2,1)S(1)} %copy-done.2, ...), custom_call_target="tpu_custom_call" | custom-call | tf_op jit(solution)/shard_map/pallas_call | solution.py:329
  81.1 0.7 copy.10
  81.8 0.6 copy.11
Async XLA Ops:
  0.6 1.0 %copy-start = (bf16[128,1024]{1,0:T(8,128)(2,1)S(1)}, bf16[128,1024]{1,0:T(8,128)(2,1)}, u32[]{:S(2)}) copy-start(bf16[128,1024]{1,0:T(8,128)(2,1)} %refs_0_.1) | copy-start | bytes 786436
  1.6 0.9 %copy-start.1 = (bf16[128,1024]{1,0:T(8,128)(2,1)S(1)}, bf16[128,1024]{1,0:T(8,128)(2,1)}, u32[]{:S(2)}) copy-start(bf16[128,1024]{1,0:T(8,128)(2,1)} %refs_3_.1) | copy-start | bytes 786436
  2.5 0.8 copy-start.2
  3.3 0.8 copy-start.3
  4.0 0.7 copy-start.4
  4.7 0.7 copy-start.5

commit v2 on v1

--- a/solution.py
+++ b/solution.py
@@ -27,11 +27,11 @@
     pairs, weights, query_rows, upstream_rows, query_t, upstream_t,
     exps, probs_grad, chunk_max, run_max, run_sum, run_dot,
     attn_low, logit_low, query_grad_t,
-    term_send, term_recv, own_sum, row_send, row_recv, gathered,
-    projected, sib_send, sib_recv, fin_send, fin_recv,
+    term_send, term_recv, own_sum, row_send, row_recv, own_low, gathered,
+    fin_send, fin_recv, query_in, upstream_in,
     gy_send, gy_recv, gu_send, gu_recv, wy_send, wy_recv,
     ru_send, ru_recv, ry_send, ry_recv, au_send, au_recv,
-    sb_send, sb_recv, fn_send, fn_recv,
+    fn_send, fn_recv, sb_send, sb_recv, in_sem,
 ):
     nu, ny, nk = sizes
     block = key_ref.shape[0]
@@ -56,7 +56,11 @@
     def y_peer(d):
         return at(u, (y + d) % ny, g)
 
+    def spread_to(d):
+        return at((u + d) % nu, y, 2 * pair + u % 2)
+
     sibling = at(u, y, g + 1 - 2 * core)
+    lead = core == u % 2
 
     def remote(src, dst, send, recv, device):
         return pltpu.make_async_remote_copy(
@@ -64,6 +68,23 @@
             device_id=device, device_id_type=MESH,
         )
 
+    own_rows = pl.ds(pl.multiple_of(s * block, block), block)
+    own_w = pl.ds(pl.multiple_of(y * wblock, wblock), wblock)
+    left, right = slice(0, HEAD), slice(HEAD, 2 * HEAD)
+    loads = [
+        pltpu.make_async_copy(src, dst, in_sem.at[i])
+        for i, (src, dst) in enumerate((
+            (key_ref, pairs.at[own_rows, left]),
+            (value_ref, pairs.at[own_rows, right]),
+            (query_ref, query_in),
+            (upstream_ref, upstream_in),
+            (key_weight_ref, weights.at[core, own_w, left]),
+            (value_weight_ref, weights.at[core, own_w, right]),
+        ))
+    ]
+    for load in loads:
+        load.start()
+
     barrier = pltpu.get_barrier_semaphore()
 
     def greet(device):
@@ -78,6 +99,13 @@
         greet(u_peer(d))
 
     greet(sibling)
+
+    @pl.loop(0, half)
+    def _(k):
+        for c in range(2):
+            @pl.when(jnp.logical_not((2 * k + core == u) & (core == c)))
+            def _():
+                greet(at(2 * k + core, y, 2 * pair + c))
 
     @pl.loop(0, nk // 2)
     def _(j):
@@ -87,17 +115,26 @@
         def _():
             greet(at(g, y, source))
 
-    own_rows = pl.ds(pl.multiple_of(s * block, block), block)
-    pairs[own_rows, :HEAD] = key_ref[...]
-    pairs[own_rows, HEAD:] = value_ref[...]
-    own_w = pl.ds(pl.multiple_of(y * wblock, wblock), wblock)
-    weights[own_w, :HEAD] = key_weight_ref[...]
-    weights[own_w, HEAD:] = value_weight_ref[...]
+    loads[0].wait()
+    loads[1].wait()
+    pl.semaphore_wait(
+        barrier, (ny - 1) + (nu - 1) + 1 + nu - jnp.where(lead, 1, 0) + half - diag
+    )
+
+    def gather_y(d):
+        return remote(pairs.at[own_rows], pairs.at[own_rows], gy_send.at[d], gy_recv.at[d], y_peer(d))
+
+    @pl.loop(1, ny)
+    def _(d):
+        gather_y(d).start()
+
+    loads[2].wait()
+    loads[3].wait()
     for h in range(heads):
         at_cols = pl.ds(h * HEAD, HEAD)
         at_rows = pl.ds(h * tokens, tokens)
-        q = query_ref[:, at_cols]
-        o = upstream_ref[:, at_cols]
+        q = query_in[:, at_cols]
+        o = upstream_in[:, at_cols]
         query_rows[at_rows, :] = q
         upstream_rows[at_rows, :] = o
         query_t[:, at_rows] = q.T
@@ -106,15 +143,8 @@
     run_sum[...] = jnp.zeros_like(run_sum)
     run_dot[...] = jnp.zeros_like(run_dot)
     query_grad_t[...] = jnp.zeros_like(query_grad_t)
-
-    pl.semaphore_wait(barrier, (ny - 1) + (nu - 1) + 1 + half - diag)
-
-    def gather_y(d):
-        return remote(pairs.at[own_rows], pairs.at[own_rows], gy_send.at[d], gy_recv.at[d], y_peer(d))
-
-    @pl.loop(1, ny)
-    def _(d):
-        gather_y(d).start()
+    loads[4].wait()
+    loads[5].wait()
 
     @pl.loop(1, ny)
     def _(d):
@@ -130,7 +160,8 @@
         gather_u(d).start()
 
     def gather_w(d):
-        return remote(weights.at[own_w], weights.at[own_w], wy_send.at[d], wy_recv.at[d], y_peer(d))
+        own = weights.at[core, own_w]
+        return remote(own, own, wy_send.at[d], wy_recv.at[d], y_peer(d))
 
     @pl.loop(1, ny)
     def _(d):
@@ -204,6 +235,15 @@
             query_grad_t[:, pl.ds(h * tokens, tokens)].T.astype(BF16)
         )
 
+    @pl.loop(1, ny)
+    def _(d):
+        gather_w(d).wait_recv()
+
+    share_w = remote(
+        weights.at[core], weights.at[core], sb_send.at[0], sb_recv.at[0], sibling
+    )
+    share_w.start()
+
     @pl.loop(1, nu)
     def _(d):
         reduce_u(d).wait_recv()
@@ -224,38 +264,44 @@
     for d in range(1, ny):
         reduce_y(d).wait_recv()
         owned += row_recv[d].astype(F32)
-    gathered[u] = owned.astype(BF16)
+    own_low[...] = owned.astype(BF16)
 
     def spread_u(d):
-        return remote(gathered.at[u], gathered.at[u], au_send.at[d], au_recv.at[d], u_peer(d))
+        return remote(
+            own_low, gathered.at[core, u // 2], au_send.at[d], au_recv.at[core * half + u // 2], spread_to(d)
+        )
+
+    @pl.when(lead)
+    def _():
+        gathered[core, u // 2] = own_low[...]
+
+    @pl.when(jnp.logical_not(lead))
+    def _():
+        spread_u(0).start()
 
     @pl.loop(1, nu)
     def _(d):
         spread_u(d).start()
 
-    @pl.loop(1, ny)
-    def _(d):
-        gather_w(d).wait_recv()
-
-    @pl.loop(1, nu)
-    def _(d):
-        spread_u(d).wait_recv()
-
-    grads = gathered[...].reshape(nu * block, 2 * HEAD)
+    share_w.wait_recv()
+
+    @pl.loop(0, half)
+    def _(k):
+        for c in range(2):
+            @pl.when(jnp.logical_not((2 * k + core == u) & (core == c)))
+            def _():
+                slot = gathered.at[c, k]
+                remote(
+                    slot, slot, au_send.at[0], au_recv.at[c * half + k], sibling
+                ).wait_recv()
+
     for n in range(ny * wblock // LANES):
         cols = pl.ds(n * LANES, LANES)
-        projected[:, cols] = contract_last(grads, weights[cols, :])
-
-    def part(j, parity):
-        return pl.ds(pl.multiple_of((2 * j + parity) * block, block), block)
-
-    def swap(j):
-        return remote(sib_send.at[j], sib_recv.at[j], sb_send.at[j], sb_recv.at[j], sibling)
-
-    @pl.loop(0, half)
-    def _(j):
-        sib_send[j] = projected[part(j, 1 - core), :].astype(BF16)
-        swap(j).start()
+        total = sum(
+            contract_last(gathered[c].reshape(half * block, 2 * HEAD), weights[c, cols, :])
+            for c in range(2)
+        )
+        fin_send[:, :, cols] = total.astype(BF16).reshape(half, block, LANES)
 
     def finish(j):
         return remote(
@@ -268,17 +314,13 @@
 
     @pl.loop(0, half)
     def _(j):
-        swap(j).wait_recv()
-        total = projected[part(j, core), :] + sib_recv[j].astype(F32)
-        fin_send[j] = total.astype(BF16)
-
         @pl.when(jnp.logical_not(to_self(j)))
         def _():
             finish(j).start()
 
         @pl.when(to_self(j))
         def _():
-            fin_recv[pair] = total.astype(BF16)
+            fin_recv[pair] = fin_send[j]
 
     @pl.loop(0, nk // 2)
     def _(j):
@@ -305,10 +347,14 @@
         reduce_u(d).wait_send()
         spread_u(d).wait_send()
 
+    @pl.when(jnp.logical_not(lead))
+    def _():
+        spread_u(0).wait_send()
+
+    share_w.wait_send()
+
     @pl.loop(0, half)
     def _(j):
-        swap(j).wait_send()
-
         @pl.when(jnp.logical_not(to_self(j)))
         def _():
             finish(j).wait_send()
@@ -332,11 +378,11 @@
             jax.ShapeDtypeStruct(text_query.shape, BF16),
             jax.ShapeDtypeStruct((block, wide), BF16),
         ),
-        in_specs=[pl.BlockSpec(memory_space=pltpu.VMEM)] * 6,
+        in_specs=[pl.BlockSpec(memory_space=pltpu.HBM)] * 6,
         out_specs=(pl.BlockSpec(memory_space=pltpu.VMEM),) * 2,
         scratch_shapes=[
             vmem((keys, 2 * HEAD), BF16),
-            vmem((wide, 2 * HEAD), BF16),
+            vmem((2, wide, 2 * HEAD), BF16),
             vmem((rows, HEAD), BF16),
             vmem((rows, HEAD), BF16),
             vmem((HEAD, rows), BF16),
@@ -355,18 +401,18 @@
             vmem((chunk, 2 * HEAD), F32),
             vmem((ny, block, 2 * HEAD), BF16),
             vmem((ny, block, 2 * HEAD), BF16),
-            vmem((nu, block, 2 * HEAD), BF16),
-            vmem((nu * block, wide), F32),
-            vmem((half, block, wide), BF16),
-            vmem((half, block, wide), BF16),
+            vmem((block, 2 * HEAD), BF16),
+            vmem((2, half, block, 2 * HEAD), BF16),
             vmem((half, block, wide), BF16),
             vmem((nk // 2, block, wide), BF16),
+            vmem(text_query.shape, BF16),
+            vmem(text_query.shape, BF16),
             dma((ny,)), dma((ny,)), dma((nu,)), dma((nu,)), dma((ny,)), dma((ny,)),
             dma((nu,)), dma((nu,)), dma((ny,)), dma((ny,)), dma((nu,)), dma((nu,)),
-            dma((half,)), dma((half,)), dma((half,)), dma((nk // 2,)),
+            dma((half,)), dma((nk // 2,)), dma((1,)), dma((1,)), dma((6,)),
         ],
         compiler_params=pltpu.CompilerParams(
-            collective_id=0, has_side_effects=True, vmem_limit_bytes=48 * 1024 * 1024
+            collective_id=0, has_side_effects=True, vmem_limit_bytes=60 * 1024 * 1024
         ),
     )(text_query, vision_key, vision_value, grad_output, key_weight, value_weight)
 

time: 82.9 us -> 77.9 us (0.940)
  local copies, waits for them, and re-layouts: 6.13 us -> 2.33 us
  Pallas kernels: 75.7 us -> 74.8 us
    unnamed x14 -> x4, local copies, waits for them, and re-layouts: 6.13 us -> 2.33 us
    pallas_call x1, Pallas kernels: 75.7 us -> 74.8 us  [shards(): pl.pallas_call(lambda *refs: kernel(sizes, *refs), out_shape=(jax.ShapeDt...]
where the time goes in v2:
time: 77.9 us; the launch traced here: 77.8 us
  Pallas kernels  74.8 us (96%)
  local copies, waits for them, and re-layouts  2.33 us (3%)
    pallas_call x1, Pallas kernels, shards(): pl.pallas_call(lambda *refs: kernel(sizes, *refs), out_shape=(jax.ShapeDt...  74.8 us
    unnamed x4, local copies, waits for them, and re-layouts  2.33 us

profile of v2, /device:TPU:71, one launch (start us, length us, event | category | flops | bytes accessed | tf_op | source)
XLA Modules:
  0.0 77.8 jit_solution(1435828612169012916)
XLA Ops:
  0.6 74.8 %shard_map.77 = (bf16[128,1024]{1,0:T(8,128)(2,1)}, bf16[32,1024]{1,0:T(8,128)(2,1)}) custom-call(bf16[128,1024]{1,0:T(8,128)(2,1)} %refs_0_.1, bf16[32,128]{1,0:T(8,128)(2,1)} %refs_1_.1, bf16[32,128]{1,0:T(8,128)(2,1)} %refs_2_.1, bf16[128,1024]{1,0:T(8,128)(2,1)} %refs_3_.1, bf16[128,128]{1,0:T(8,128)(2,1)} %refs_4_.1, bf16[128,128]{1,0:T(8,128)(2,1)} %refs_5_.1), custom_call_target="tpu_custom_call" | custom-call | tf_op jit(solution)/shard_map/pallas_call | solution.py:375
  75.4 0.0 copy-start
  75.4 1.7 %copy.10 = bf16[128,1024]{1,0:T(8,128)(2,1)} copy(bf16[128,1024]{1,0:T(8,128)(2,1)} %get-tuple-element.4) | data formatting | bytes 524288
  77.1 0.0 copy-done
  77.1 0.6 copy.11
Async XLA Ops:
  75.4 1.7 %copy-start = (bf16[32,1024]{1,0:T(8,128)(2,1)S(1)}, bf16[32,1024]{1,0:T(8,128)(2,1)}, u32[]{:S(2)}) copy-start(bf16[32,1024]{1,0:T(8,128)(2,1)} %get-tuple-element.5) | copy-start | bytes 196612

commit v3 on v2

--- a/solution.py
+++ b/solution.py
@@ -11,6 +11,7 @@
 SCALING = 1.0 / math.sqrt(HEAD)
 EXP2_SCALE = SCALING * math.log2(math.e)
 LANES = 256
+PARTS = 2
 MESH = pl.DeviceIdType.MESH
 F32 = jnp.float32
 BF16 = jnp.bfloat16
@@ -68,7 +69,16 @@
             device_id=device, device_id_type=MESH,
         )
 
-    own_rows = pl.ds(pl.multiple_of(s * block, block), block)
+    order = [0]
+    for step in range(1, ny // 2 + 1):
+        order += [r for r in (step, ny - step) if r not in order]
+    groups = [(0, 1), (1, min(3, ny)), (min(3, ny), ny)]
+    groups = [(lo, hi) for lo, hi in groups if hi > lo]
+
+    def slots(lo, hi):
+        return pl.ds(pl.multiple_of(u * chunk + lo * block, block), (hi - lo) * block)
+
+    own_rows = slots(0, 1)
     own_w = pl.ds(pl.multiple_of(y * wblock, wblock), wblock)
     left, right = slice(0, HEAD), slice(HEAD, 2 * HEAD)
     loads = [
@@ -102,10 +112,9 @@
 
     @pl.loop(0, half)
     def _(k):
-        for c in range(2):
-            @pl.when(jnp.logical_not((2 * k + core == u) & (core == c)))
-            def _():
-                greet(at(2 * k + core, y, 2 * pair + c))
+        @pl.when(2 * k + core != u)
+        def _():
+            greet(at(2 * k + core, y, g + 1 - 2 * core))
 
     @pl.loop(0, nk // 2)
     def _(j):
@@ -118,15 +127,25 @@
     loads[0].wait()
     loads[1].wait()
     pl.semaphore_wait(
-        barrier, (ny - 1) + (nu - 1) + 1 + nu - jnp.where(lead, 1, 0) + half - diag
+        barrier, (ny - 1) + (nu - 1) + 1 + jnp.where(lead, 0, nu - 1) + half - diag
     )
 
     def gather_y(d):
-        return remote(pairs.at[own_rows], pairs.at[own_rows], gy_send.at[d], gy_recv.at[d], y_peer(d))
-
-    @pl.loop(1, ny)
-    def _(d):
-        gather_y(d).start()
+        i = order.index(ny - d)
+        return remote(
+            pairs.at[own_rows], pairs.at[slots(i, i + 1)], gy_send.at[d], gy_recv.at[d], y_peer(d)
+        )
+
+    def gather_u(d, k):
+        part = pairs.at[slots(*groups[k])]
+        return remote(part, part, gu_send.at[k, d], gu_recv.at[k, d], u_peer(d))
+
+    for i in reversed(range(1, ny)):
+        gather_y(order[i]).start()
+
+    @pl.loop(1, nu)
+    def _(d):
+        gather_u(d, 0).start()
 
     loads[2].wait()
     loads[3].wait()
@@ -146,18 +165,13 @@
     loads[4].wait()
     loads[5].wait()
 
-    @pl.loop(1, ny)
-    def _(d):
-        gather_y(d).wait_recv()
-
-    u_rows = pl.ds(pl.multiple_of(u * chunk, chunk), chunk)
-
-    def gather_u(d):
-        return remote(pairs.at[u_rows], pairs.at[u_rows], gu_send.at[d], gu_recv.at[d], u_peer(d))
-
-    @pl.loop(1, nu)
-    def _(d):
-        gather_u(d).start()
+    for k, (lo, hi) in enumerate(groups[1:], 1):
+        for i in range(lo, hi):
+            gather_y(ny - order[i]).wait_recv()
+
+        @pl.loop(1, nu)
+        def _(d):
+            gather_u(d, k).start()
 
     def gather_w(d):
         own = weights.at[core, own_w]
@@ -171,7 +185,8 @@
     def _(d):
         @pl.when(d > 0)
         def _():
-            gather_u(d).wait_recv()
+            for k in range(len(groups)):
+                gather_u(d, k).wait_recv()
 
         c = (u - d + nu) % nu
         at_c = pl.ds(pl.multiple_of(c * chunk, chunk), chunk)
@@ -195,13 +210,22 @@
     run_sum[...] = 1.0 / run_sum[...]
     run_dot[...] = run_dot[...] * run_sum[...]
 
-    def reduce_u(d):
-        return remote(term_send.at[d], term_recv.at[d], ru_send.at[d], ru_recv.at[d], u_peer(d))
-
-    @pl.loop(1, nu + 1)
-    def _(d):
+    span = chunk // PARTS
+
+    def reduce_u(d, h):
+        rows_h = pl.ds(pl.multiple_of(h * span, span), span)
+        return remote(
+            term_send.at[d, rows_h], term_recv.at[d, rows_h],
+            ru_send.at[h, d], ru_recv.at[h, d], u_peer(d),
+        )
+
+    @pl.loop(0, PARTS * nu)
+    def _(t):
+        h = PARTS - 1 - t // nu
+        d = 1 + t % nu
         c = (u + d) % nu
-        at_c = pl.ds(pl.multiple_of(c * chunk, chunk), chunk)
+        at_h = pl.ds(pl.multiple_of(h * span, span), span)
+        at_c = pl.ds(pl.multiple_of(c * chunk + h * span, span), span)
         for n in range(rows // LANES):
             cols = pl.ds(n * LANES, LANES)
             share = (
@@ -218,16 +242,16 @@
 
         @pl.when(d < nu)
         def _():
-            term_send[d, :, :HEAD] = key_term.astype(BF16)
-            term_send[d, :, HEAD:] = value_term.astype(BF16)
-            reduce_u(d).start()
+            term_send[d, at_h, left] = key_term.astype(BF16)
+            term_send[d, at_h, right] = value_term.astype(BF16)
+            reduce_u(d, h).start()
 
         @pl.when(d == nu)
         def _():
-            own_sum[:, :HEAD] = key_term
-            own_sum[:, HEAD:] = value_term
-
-        keys_t = pairs[at_c, :HEAD].T
+            own_sum[at_h, left] = key_term
+            own_sum[at_h, right] = value_term
+
+        keys_t = pairs[at_c, left].T
         query_grad_t[...] += jnp.dot(keys_t, logit_low[...], preferred_element_type=F32)
 
     for h in range(heads):
@@ -244,24 +268,24 @@
     )
     share_w.start()
 
-    @pl.loop(1, nu)
-    def _(d):
-        reduce_u(d).wait_recv()
-        own_sum[...] += term_recv[d].astype(F32)
-
     def reduce_y(d):
         return remote(row_send.at[d], row_recv.at[d], ry_send.at[d], ry_recv.at[d], y_peer(d))
 
-    def y_rows(d):
-        return pl.ds(pl.multiple_of(((y + d) % ny) * block, block), block)
-
-    @pl.loop(1, ny)
-    def _(d):
-        row_send[d] = own_sum[y_rows(d), :].astype(BF16)
-        reduce_y(d).start()
-
-    owned = own_sum[y_rows(0), :]
-    for d in range(1, ny):
+    for h in reversed(range(PARTS)):
+        at_h = pl.ds(h * span, span)
+
+        @pl.loop(1, nu)
+        def _(d):
+            reduce_u(d, h).wait_recv()
+            own_sum[at_h, :] += term_recv[d, at_h, :].astype(F32)
+
+        for i in reversed(range(max(h * ny // PARTS, 1), (h + 1) * ny // PARTS)):
+            row_send[order[i]] = own_sum[pl.ds(i * block, block), :].astype(BF16)
+            reduce_y(order[i]).start()
+
+    owned = own_sum[pl.ds(0, block), :]
+    for i in range(1, ny):
+        d = order[i]
         reduce_y(d).wait_recv()
         owned += row_recv[d].astype(F32)
     own_low[...] = owned.astype(BF16)
@@ -335,16 +359,17 @@
         result += fin_recv[j].astype(F32)
     grad_vision_ref[...] = result.astype(BF16)
 
-    @pl.loop(1, ny)
-    def _(d):
+    for d in range(1, ny):
         gather_y(d).wait_send()
         gather_w(d).wait_send()
         reduce_y(d).wait_send()
 
     @pl.loop(1, nu)
     def _(d):
-        gather_u(d).wait_send()
-        reduce_u(d).wait_send()
+        for k in range(len(groups)):
+            gather_u(d, k).wait_send()
+        for h in range(PARTS):
+            reduce_u(d, h).wait_send()
         spread_u(d).wait_send()
 
     @pl.when(jnp.logical_not(lead))
@@ -393,8 +418,8 @@
             vmem((1, rows), F32),
             vmem((1, rows), F32),
             vmem((1, rows), F32),
-            vmem((chunk, rows), BF16),
-            vmem((chunk, rows), BF16),
+            vmem((chunk // PARTS, rows), BF16),
+            vmem((chunk // PARTS, rows), BF16),
             vmem((HEAD, rows), F32),
             vmem((nu, chunk, 2 * HEAD), BF16),
             vmem((nu, chunk, 2 * HEAD), BF16),
@@ -407,8 +432,8 @@
             vmem((nk // 2, block, wide), BF16),
             vmem(text_query.shape, BF16),
             vmem(text_query.shape, BF16),
-            dma((ny,)), dma((ny,)), dma((nu,)), dma((nu,)), dma((ny,)), dma((ny,)),
-            dma((nu,)), dma((nu,)), dma((ny,)), dma((ny,)), dma((nu,)), dma((nu,)),
+            dma((ny,)), dma((ny,)), dma((3, nu)), dma((3, nu)), dma((ny,)), dma((ny,)),
+            dma((PARTS, nu)), dma((PARTS, nu)), dma((ny,)), dma((ny,)), dma((nu,)), dma((nu,)),
             dma((half,)), dma((nk // 2,)), dma((1,)), dma((1,)), dma((6,)),
         ],
         compiler_params=pltpu.CompilerParams(

time: 77.9 us -> 72.5 us (0.931)
  the two profiles are of different devices: /device:TPU:71 before, /device:TPU:68 now
where the time goes in v3:
time: 72.5 us; the launch traced here: 72.4 us
  Pallas kernels  69.4 us (96%)
  local copies, waits for them, and re-layouts  2.33 us (3%)
    pallas_call x1, Pallas kernels, shards(): pl.pallas_call(lambda *refs: kernel(sizes, *refs), out_shape=(jax.ShapeDt...  69.4 us
    unnamed x4, local copies, waits for them, and re-layouts  2.33 us

profile of v3, /device:TPU:68, one launch (start us, length us, event | category | flops | bytes accessed | tf_op | source)
XLA Modules:
  0.0 72.4 jit_solution(8157188603239170588)
XLA Ops:
  0.6 69.4 %shard_map.77 = (bf16[128,1024]{1,0:T(8,128)(2,1)}, bf16[32,1024]{1,0:T(8,128)(2,1)}) custom-call(bf16[128,1024]{1,0:T(8,128)(2,1)} %refs_0_.1, bf16[32,128]{1,0:T(8,128)(2,1)} %refs_1_.1, bf16[32,128]{1,0:T(8,128)(2,1)} %refs_2_.1, bf16[128,1024]{1,0:T(8,128)(2,1)} %refs_3_.1, bf16[128,128]{1,0:T(8,128)(2,1)} %refs_4_.1, bf16[128,128]{1,0:T(8,128)(2,1)} %refs_5_.1), custom_call_target="tpu_custom_call" | custom-call | tf_op jit(solution)/shard_map/pallas_call | solution.py:400
  70.0 0.0 copy-start
  70.1 1.7 %copy.10 = bf16[128,1024]{1,0:T(8,128)(2,1)} copy(bf16[128,1024]{1,0:T(8,128)(2,1)} %get-tuple-element.4) | data formatting | bytes 524288
  71.8 0.0 copy-done
  71.8 0.6 copy.11
Async XLA Ops:
  70.0 1.7 %copy-start = (bf16[32,1024]{1,0:T(8,128)(2,1)S(1)}, bf16[32,1024]{1,0:T(8,128)(2,1)}, u32[]{:S(2)}) copy-start(bf16[32,1024]{1,0:T(8,128)(2,1)} %get-tuple-element.5) | copy-start | bytes 196612

commit v4 on v3

--- a/solution.py
+++ b/solution.py
@@ -12,6 +12,8 @@
 EXP2_SCALE = SCALING * math.log2(math.e)
 LANES = 256
 PARTS = 2
+STEP_IN = 1
+STEP_OUT = 5
 MESH = pl.DeviceIdType.MESH
 F32 = jnp.float32
 BF16 = jnp.bfloat16
@@ -100,12 +102,10 @@
     def greet(device):
         pl.semaphore_signal(barrier, inc=1, device_id=device, device_id_type=MESH)
 
-    @pl.loop(1, ny)
-    def _(d):
+    for d in range(1, ny):
         greet(y_peer(d))
 
-    @pl.loop(1, nu)
-    def _(d):
+    for d in range(1, nu):
         greet(u_peer(d))
 
     greet(sibling)
@@ -143,9 +143,8 @@
     for i in reversed(range(1, ny)):
         gather_y(order[i]).start()
 
-    @pl.loop(1, nu)
-    def _(d):
-        gather_u(d, 0).start()
+    for d in range(1, nu):
+        gather_u(STEP_IN * d % nu, 0).start()
 
     loads[2].wait()
     loads[3].wait()
@@ -169,9 +168,8 @@
         for i in range(lo, hi):
             gather_y(ny - order[i]).wait_recv()
 
-        @pl.loop(1, nu)
-        def _(d):
-            gather_u(d, k).start()
+        for d in range(1, nu):
+            gather_u(STEP_IN * d % nu, k).start()
 
     def gather_w(d):
         own = weights.at[core, own_w]
@@ -182,8 +180,10 @@
         gather_w(d).start()
 
     @pl.loop(0, nu)
-    def _(d):
-        @pl.when(d > 0)
+    def _(turn):
+        d = STEP_IN * turn % nu
+
+        @pl.when(turn > 0)
         def _():
             for k in range(len(groups)):
                 gather_u(d, k).wait_recv()
@@ -222,7 +222,8 @@
     @pl.loop(0, PARTS * nu)
     def _(t):
         h = PARTS - 1 - t // nu
-        d = 1 + t % nu
+        turn = 1 + t % nu
+        d = jnp.where(turn == nu, nu, STEP_OUT * turn % nu)
         c = (u + d) % nu
         at_h = pl.ds(pl.multiple_of(h * span, span), span)
         at_c = pl.ds(pl.multiple_of(c * chunk + h * span, span), span)
@@ -275,7 +276,8 @@
         at_h = pl.ds(h * span, span)
 
         @pl.loop(1, nu)
-        def _(d):
+        def _(turn):
+            d = STEP_OUT * turn % nu
             reduce_u(d, h).wait_recv()
             own_sum[at_h, :] += term_recv[d, at_h, :].astype(F32)
 
@@ -303,8 +305,7 @@
     def _():
         spread_u(0).start()
 
-    @pl.loop(1, nu)
-    def _(d):
+    for d in range(1, nu):
         spread_u(d).start()
 
     share_w.wait_recv()

time: 72.5 us -> 71.4 us (0.985)
  Pallas kernels: 69.4 us -> 68.2 us
    pallas_call x1, Pallas kernels: 69.4 us -> 68.2 us  [shards(): pl.pallas_call(lambda *refs: kernel(sizes, *refs), out_shape=(jax.ShapeDt...]
where the time goes in v4:
time: 71.4 us; the launch traced here: 71.2 us
  Pallas kernels  68.2 us (96%)
  local copies, waits for them, and re-layouts  2.33 us (3%)
    pallas_call x1, Pallas kernels, shards(): pl.pallas_call(lambda *refs: kernel(sizes, *refs), out_shape=(jax.ShapeDt...  68.2 us
    unnamed x4, local copies, waits for them, and re-layouts  2.33 us

profile of v4, /device:TPU:68, one launch (start us, length us, event | category | flops | bytes accessed | tf_op | source)
XLA Modules:
  0.0 71.2 jit_solution(13301519276560635415)
XLA Ops:
  0.6 68.2 %shard_map.77 = (bf16[128,1024]{1,0:T(8,128)(2,1)}, bf16[32,1024]{1,0:T(8,128)(2,1)}) custom-call(bf16[128,1024]{1,0:T(8,128)(2,1)} %refs_0_.1, bf16[32,128]{1,0:T(8,128)(2,1)} %refs_1_.1, bf16[32,128]{1,0:T(8,128)(2,1)} %refs_2_.1, bf16[128,1024]{1,0:T(8,128)(2,1)} %refs_3_.1, bf16[128,128]{1,0:T(8,128)(2,1)} %refs_4_.1, bf16[128,128]{1,0:T(8,128)(2,1)} %refs_5_.1), custom_call_target="tpu_custom_call" | custom-call | tf_op jit(solution)/shard_map/pallas_call | solution.py:401
  68.9 0.0 copy-start
  68.9 1.7 %copy.10 = bf16[128,1024]{1,0:T(8,128)(2,1)} copy(bf16[128,1024]{1,0:T(8,128)(2,1)} %get-tuple-element.4) | data formatting | bytes 524288
  70.6 0.0 copy-done
  70.6 0.6 copy.11
Async XLA Ops:
  68.9 1.7 %copy-start = (bf16[32,1024]{1,0:T(8,128)(2,1)S(1)}, bf16[32,1024]{1,0:T(8,128)(2,1)}, u32[]{:S(2)}) copy-start(bf16[32,1024]{1,0:T(8,128)(2,1)} %get-tuple-element.5) | copy-start | bytes 196612

commit v5 on v4

--- a/solution.py
+++ b/solution.py
@@ -12,7 +12,7 @@
 EXP2_SCALE = SCALING * math.log2(math.e)
 LANES = 256
 PARTS = 2
-STEP_IN = 1
+STEP_IN = 5
 STEP_OUT = 5
 MESH = pl.DeviceIdType.MESH
 F32 = jnp.float32

time: 71.4 us -> 71.4 us (level)
  no operation moved by 1% of the time
where the time goes in v5:
time: 71.4 us; the launch traced here: 71.2 us
  Pallas kernels  68.3 us (96%)
  local copies, waits for them, and re-layouts  2.33 us (3%)
    pallas_call x1, Pallas kernels, shards(): pl.pallas_call(lambda *refs: kernel(sizes, *refs), out_shape=(jax.ShapeDt...  68.3 us
    unnamed x4, local copies, waits for them, and re-layouts  2.33 us

profile of v5, /device:TPU:68, one launch (start us, length us, event | category | flops | bytes accessed | tf_op | source)
XLA Modules:
  0.0 71.2 jit_solution(3856782585908812112)
XLA Ops:
  0.6 68.3 %shard_map.77 = (bf16[128,1024]{1,0:T(8,128)(2,1)}, bf16[32,1024]{1,0:T(8,128)(2,1)}) custom-call(bf16[128,1024]{1,0:T(8,128)(2,1)} %refs_0_.1, bf16[32,128]{1,0:T(8,128)(2,1)} %refs_1_.1, bf16[32,128]{1,0:T(8,128)(2,1)} %refs_2_.1, bf16[128,1024]{1,0:T(8,128)(2,1)} %refs_3_.1, bf16[128,128]{1,0:T(8,128)(2,1)} %refs_4_.1, bf16[128,128]{1,0:T(8,128)(2,1)} %refs_5_.1), custom_call_target="tpu_custom_call" | custom-call | tf_op jit(solution)/shard_map/pallas_call | solution.py:401
  68.9 0.0 copy-start
  68.9 1.7 %copy.10 = bf16[128,1024]{1,0:T(8,128)(2,1)} copy(bf16[128,1024]{1,0:T(8,128)(2,1)} %get-tuple-element.4) | data formatting | bytes 524288
  70.6 0.0 copy-done
  70.6 0.6 copy.11
Async XLA Ops:
  68.9 1.7 %copy-start = (bf16[32,1024]{1,0:T(8,128)(2,1)S(1)}, bf16[32,1024]{1,0:T(8,128)(2,1)}, u32[]{:S(2)}) copy-start(bf16[32,1024]{1,0:T(8,128)(2,1)} %get-tuple-element.5) | copy-start | bytes 196612
